TPU v7x, 32 devices: a whole 2x2x4 slice. The times are simulated.
32 devices in a mesh: row: 8 (over z, core), col: 4 (over y, x), rep: 1.
Axes of the slice: x: 2, y: 2, z: 4, core: 2. Of those that a mesh axis runs over, the one named last changes fastest.
Arguments:
- momentum: float32 [1, 8192, 8192], P('rep', 'row', 'col'), may hold values from -6 to 6
- gradient: bfloat16 [1, 8192, 8192], P('rep', 'row', 'col'), may hold values from -6 to 6
- weight: float32 [8192, 8192], P('row', 'col'), may hold values from -0.0625 to 0.0625
- right_basis: float32 [8192, 256], P('col'), may hold values from -6 to 6
Outputs:
- new_momentum: float32 [1, 8192, 8192], P('rep', 'row', 'col')
- new_weight: float32 [8192, 8192], P('row', 'col')
- new_basis: float32 [8192, 256], P('col')
All inputs are finite; a program needn't handle non-finite values.
Results may differ from a plain program's by a relative error of at most 0.0012.
Values sent between devices are 32-bit elements; how exact they have to be, the bound alone decides.
No kernel may reach another device: no remote copies, remote signals or barrier semaphores. Data moves between devices by JAX's collectives and lax.ppermute only.
A program may use at most 128 MiB of HBM per device.

v0:
```python
import jax
import jax.numpy as jnp
from jax import lax
from jax.sharding import PartitionSpec as P

D = 8192
RANK = 256
ITERS = 2


beta_mom = 0.95
learn_rate = 0.05


def on_device(momentum, gradient, weight, right_basis):
    highest = lax.Precision.HIGHEST
    replicas = lax.axis_size("rep")
    buffer = momentum[0] + gradient[0].astype(jnp.float32)
    basis_now = right_basis
    ortho = None
    factor = None
    for sweep in range(ITERS):
        left_part = (
            jnp.dot(buffer, basis_now, precision=highest, preferred_element_type=jnp.float32)
            / replicas
        )
        left = lax.psum(left_part, ("col", "rep"))
        gram_part = jnp.dot(left.T, left, precision=highest, preferred_element_type=jnp.float32)
        gram_full = lax.psum(gram_part, "row")
        low_factor = jnp.linalg.cholesky(gram_full)
        ortho = jax.scipy.linalg.solve_triangular(low_factor, left.T, lower=True).T
        factor_part = (
            jnp.dot(buffer.T, ortho, precision=highest, preferred_element_type=jnp.float32)
            / replicas
        )
        wide_piece = lax.psum_scatter(factor_part, ("row", "rep"), scatter_dimension=0, tiled=True)
        square_sum = lax.psum(jnp.sum(wide_piece * wide_piece, axis=0), ("row", "col", "rep"))
        factor = lax.all_gather(wide_piece, ("row", "rep"), axis=0, tiled=True)
        rms_cols = jnp.sqrt(square_sum / jnp.float32(D) + 1e-06)
        basis_now = factor / rms_cols
    feedback = jnp.dot(ortho, factor.T, precision=highest, preferred_element_type=jnp.float32)
    new_momentum = (buffer - (1.0 - beta_mom) * feedback)[None]
    update = jnp.dot(ortho, basis_now.T, precision=highest, preferred_element_type=jnp.float32)
    new_weight = weight - learn_rate * jnp.sqrt(jnp.float32(D) / jnp.float32(RANK)) * update
    return (new_momentum, new_weight, basis_now)


def solution(mesh):
    return jax.shard_map(
        on_device,
        mesh=mesh,
        in_specs=(P("rep", "row", "col"), P("rep", "row", "col"), P("row", "col"), P("col", None)),
        out_specs=(P("rep", "row", "col"), P("row", "col"), P("col", None)),
        check_vma=False,
    )
```

profile of v0, /device:TPU:0, one launch (start us, length us, event | category | flops | bytes accessed | tf_op | source)
XLA Modules:
  0.0 620.8 jit_solution(1863495676450695879)
XLA Ops:
  8.8 10.7 %fusion.6 = f32[1024,256]{1,0:T(8,128)} fusion(f32[2048,256]{1,0:T(8,128)S(1)} %copy-done, f32[1,1024,2048]{2,1,0:T(8,128)} %param.7, bf16[1,1024,2048]{2,1,0:T(8,128)(2,1)} %param.8), kind=kOutput, calls=%fused_computation.11 | convolution fusion | flops 6446645248 | bytes 15728640 | tf_op jit(solution)/shard_map/dot_general | solution.py:24
  19.6 55.4 %all-reduce.6.cloned.1.call-done = f32[1024,256]{1,0:T(8,128)} async-done(((f32[1024,256]{1,0:T(8,128)}), f32[1024,256]{1,0:T(8,128)}) %all-reduce.6.cloned.1.call-update) | async-done | bytes 1048592 | tf_op jit(solution)/shard_map/psum | solution.py:27
  79.4 54.7 %all-reduce.8.cloned.1.call-done = f32[256,256]{0,1:T(8,128)} async-done(((f32[256,256]{0,1:T(8,128)}), f32[256,256]{0,1:T(8,128)}) %all-reduce.8.cloned.1.call-update) | async-done | bytes 262160 | tf_op jit(solution)/shard_map/psum | solution.py:29
  136.2 11.7 %cholesky.130 = f32[128,128]{1,0:T(8,128)S(1)} custom-call(f32[128,128]{1,0:T(8,128)S(1)} %cholesky.194), custom_call_target="Cholesky" | custom-call | tf_op jit(solution)/shard_map/jit(cholesky)/cholesky | solution.py:30
  147.9 9.8 %custom-call.13 = f32[1,128,128]{1,2,0:T(8,128)S(1)} custom-call(f32[1,128,128]{2,1,0:T(8,128)S(1)} %get-tuple-element.48), custom_call_target="InvertDiagBlocksLowerTriangular" | custom-call | tf_op jit(solution)/shard_map/jit(cholesky)/cholesky | solution.py:30
  158.2 11.7 %cholesky.147 = f32[128,128]{1,0:T(8,128)S(1)} custom-call(f32[128,128]{1,0:T(8,128)S(1)} %convolution_subtract_fusion.3), custom_call_target="Cholesky" | custom-call | tf_op jit(solution)/shard_map/jit(cholesky)/cholesky | solution.py:30
  172.2 4.6 while.4
  176.8 19.7 %custom-call.14 = f32[2,128,128]{1,2,0:T(8,128)S(1)} custom-call(f32[2,128,128]{2,1,0:T(8,128)S(1)} %get-tuple-element.19), custom_call_target="InvertDiagBlocksLowerTriangular" | custom-call | tf_op jit(solution)/shard_map/jit(_solve_triangular)/triangular_solve | solution.py:31
  200.9 17.3 %fusion.4 = f32[2048,256]{1,0:T(8,128)} fusion(f32[128,1024]{1,0:T(8,128)S(1)} %fusion.25, f32[128,1024]{1,0:T(8,128)S(1)} %fusion.16, f32[1,1024,2048]{2,1,0:T(8,128)} %param.7, bf16[1,1024,2048]{2,1,0:T(8,128)(2,1)} %param.8), kind=kOutput, calls=%fused_computation.9 | convolution fusion | flops 6446907392 | bytes 15728640 | tf_op jit(solution)/shard_map/dot_general | solution.py:33
  218.2 34.9 %reduce-scatter.3.cloned.1.call-done = f32[256,256]{1,0:T(8,128)} async-done(((f32[2048,256]{1,0:T(8,128)}), f32[256,256]{1,0:T(8,128)}) %reduce-scatter.3.cloned.1.call-update) | async-done | bytes 262160 | tf_op jit(solution)/shard_map/reduce_scatter | solution.py:36
  254.2 39.0 %psum.44 = f32[256]{0:T(256)S(1)} all-reduce(f32[256]{0:T(256)S(1)} %multiply_reduce_fusion.1), channel_id=1, replica_groups=mesh['row'=8,'col'=4,'rep'=1] {'row','col','rep'}, use_global_device_ids=true, to_apply=%region_8.0 | all-reduce | flops 256 | bytes 2048 | tf_op jit(solution)/shard_map/psum | solution.py:37
  293.2 11.6 %fusion.2 = f32[1024,256]{1,0:T(8,128)} fusion(f32[2048,256]{1,0:T(8,128)} %all-gather.3.cloned.1.call-done, f32[256]{0:T(256)S(1)} %add_sqrt_fusion.1, f32[1,1024,2048]{2,1,0:T(8,128)} %param.7, bf16[1,1024,2048]{2,1,0:T(8,128)(2,1)} %param.8), kind=kOutput, calls=%fused_computation.7 | convolution fusion | flops 6447169536 | bytes 15729664 | tf_op jit(solution)/shard_map/dot_general | solution.py:24
  304.9 53.2 %all-reduce.10.cloned.1.call-done = f32[1024,256]{1,0:T(8,128)} async-done(((f32[1024,256]{1,0:T(8,128)}), f32[1024,256]{1,0:T(8,128)}) %all-reduce.10.cloned.1.call-update) | async-done | bytes 1048592 | tf_op jit(solution)/shard_map/psum | solution.py:27
  362.4 54.8 %all-reduce.12.cloned.1.call-done = f32[256,256]{0,1:T(8,128)} async-done(((f32[256,256]{0,1:T(8,128)}), f32[256,256]{0,1:T(8,128)}) %all-reduce.12.cloned.1.call-update) | async-done | bytes 262160 | tf_op jit(solution)/shard_map/psum | solution.py:29
  419.2 11.7 %cholesky.164 = f32[128,128]{1,0:T(8,128)S(1)} custom-call(f32[128,128]{1,0:T(8,128)S(1)} %cholesky.197), custom_call_target="Cholesky" | custom-call | tf_op jit(solution)/shard_map/jit(cholesky)/cholesky | solution.py:30
  431.6 9.8 %custom-call.15 = f32[1,128,128]{1,2,0:T(8,128)S(1)} custom-call(f32[1,128,128]{2,1,0:T(8,128)S(1)} %get-tuple-element.44), custom_call_target="InvertDiagBlocksLowerTriangular" | custom-call | tf_op jit(solution)/shard_map/jit(cholesky)/cholesky | solution.py:30
  442.0 11.7 %cholesky.181 = f32[128,128]{1,0:T(8,128)S(1)} custom-call(f32[128,128]{1,0:T(8,128)S(1)} %convolution_subtract_fusion.2), custom_call_target="Cholesky" | custom-call | tf_op jit(solution)/shard_map/jit(cholesky)/cholesky | solution.py:30
  455.7 4.3 while.5
  460.0 19.7 %custom-call.16 = f32[2,128,128]{1,2,0:T(8,128)S(1)} custom-call(f32[2,128,128]{2,1,0:T(8,128)S(1)} %get-tuple-element.20), custom_call_target="InvertDiagBlocksLowerTriangular" | custom-call | tf_op jit(solution)/shard_map/jit(_solve_triangular)/triangular_solve | solution.py:31
  484.0 17.2 %fusion = f32[2048,256]{1,0:T(8,128)} fusion(f32[128,1024]{1,0:T(8,128)S(1)} %fusion.21, f32[128,1024]{1,0:T(8,128)S(1)} %fusion.14, f32[1,1024,2048]{2,1,0:T(8,128)} %param.7, bf16[1,1024,2048]{2,1,0:T(8,128)(2,1)} %param.8), kind=kOutput, calls=%fused_computation.5 | convolution fusion | flops 6446907392 | bytes 15728640 | tf_op jit(solution)/shard_map/dot_general | solution.py:33
  501.3 34.8 %reduce-scatter.5.cloned.1.call-done = f32[256,256]{1,0:T(8,128)} async-done(((f32[2048,256]{1,0:T(8,128)}), f32[256,256]{1,0:T(8,128)}) %reduce-scatter.5.cloned.1.call-update) | async-done | bytes 262160 | tf_op jit(solution)/shard_map/reduce_scatter | solution.py:36
  537.2 39.7 %psum.47 = f32[256]{0:T(256)S(1)} all-reduce(f32[256]{0:T(256)S(1)} %multiply_reduce_fusion), channel_id=1, replica_groups=mesh['row'=8,'col'=4,'rep'=1] {'row','col','rep'}, use_global_device_ids=true, to_apply=%region_13.16 | all-reduce | flops 256 | bytes 2048 | tf_op jit(solution)/shard_map/psum | solution.py:37
  578.8 18.5 %multiply_subtract_fusion = f32[1024,2048]{1,0:T(8,128)} fusion(f32[1024,2048]{1,0:T(8,128)} %param.9, f32[2048,256]{1,0:T(8,128)S(1)} %broadcast_divide_fusion, f32[128,1024]{1,0:T(8,128)S(1)} %fusion.21, f32[128,1024]{1,0:T(8,128)S(1)} %fusion.14), kind=kOutput, calls=%fused_computation.14 | convolution fusion | flops 6446907392 | bytes 19922944 | tf_op jit(solution)/shard_map/dot_general | solution.py:43
  597.3 16.4 %fusion.8 = f32[1,1024,2048]{2,1,0:T(8,128)} fusion(f32[2048,256]{1,0:T(8,128)S(1)} %copy-done.2, f32[128,1024]{1,0:T(8,128)S(1)} %fusion.21, f32[128,1024]{1,0:T(8,128)S(1)} %fusion.14, f32[1,1024,2048]{2,1,0:T(8,128)S(1)} %bitcast.86, bf16[1,1024,2048]{2,1,0:T(8,128)(2,1)S(1)} %copy-done.1), kind=kOutput, calls=%fused_computation.13 | convolution fusion | flops 6451101696 | bytes 24117248 | tf_op jit(solution)/shard_map/dot_general | solution.py:41
  (81 shorter events, 38.7 us)
Async XLA Ops:
  7.2 1.6 copy-start
  7.2 67.7 %all-reduce.6.cloned.1.call-start = ((), (), s32[]{:S(2)}) async-start(), calls=%async_computation.2 | async-start | bytes 2097152 | tf_op jit(solution)/shard_map/psum | solution.py:27
  19.5 114.6 %all-reduce.8.cloned.1.call-start = ((), (), s32[]{:S(2)}) async-start(), calls=%async_computation.3 | async-start | bytes 524288 | tf_op jit(solution)/shard_map/psum | solution.py:29
  79.0 174.1 %reduce-scatter.3.cloned.1.call-start = ((), (), s32[]{:S(2)}) async-start(), calls=%async_computation.4 | async-start | bytes 2359296 | tf_op jit(solution)/shard_map/reduce_scatter | solution.py:36
  218.2 75.1 %all-gather.3.cloned.1.call-start = ((), (), s32[]{:S(2)}) async-start(), calls=%async_computation.5 | async-start | bytes 2359296 | tf_op jit(solution)/shard_map/all_gather | solution.py:38
  253.1 104.9 %all-reduce.10.cloned.1.call-start = ((), (), s32[]{:S(2)}) async-start(), calls=%async_computation.6 | async-start | bytes 2097152 | tf_op jit(solution)/shard_map/psum | solution.py:27
  304.8 112.3 %all-reduce.12.cloned.1.call-start = ((), (), s32[]{:S(2)}) async-start(), calls=%async_computation.7 | async-start | bytes 524288 | tf_op jit(solution)/shard_map/psum | solution.py:29
  362.1 174.0 %reduce-scatter.5.cloned.1.call-start = ((), (), s32[]{:S(2)}) async-start(), calls=%async_computation.8 | async-start | bytes 2359296 | tf_op jit(solution)/shard_map/reduce_scatter | solution.py:36
  501.3 75.6 %all-gather.5.cloned.1.call-start = ((), (), s32[]{:S(2)}) async-start(), calls=%async_computation.9 | async-start | bytes 2359296 | tf_op jit(solution)/shard_map/all_gather | solution.py:38
  576.9 20.4 %slice-start = ((s8[8388608]{0:T(1024)(128)(4,1)}), s8[4194304]{0:T(1024)(128)(4,1)S(1)}, s32[]{:S(2)}) async-start(s8[8388608]{0:T(1024)(128)(4,1)} %bitcast.85), calls=%async_computation.10 | async-start | bytes 8388608
  578.8 18.5 %copy-start.3 = (f32[2048,256]{1,0:T(8,128)}, f32[2048,256]{1,0:T(8,128)S(1)}, u32[]{:S(2)}) copy-start(f32[2048,256]{1,0:T(8,128)S(1)} %broadcast_divide_fusion) | copy-start | bytes 6291460
  578.8 18.5 %slice-start.1 = ((s8[8388608]{0:T(1024)(128)(4,1)}), s8[4194304]{0:T(1024)(128)(4,1)S(1)}, s32[]{:S(2)}) async-start(s8[8388608]{0:T(1024)(128)(4,1)} %bitcast.85), calls=%async_computation.11 | async-start | bytes 8388608
  578.8 18.5 %copy-start.1 = (bf16[1,1024,2048]{2,1,0:T(8,128)(2,1)S(1)}, bf16[1,1024,2048]{2,1,0:T(8,128)(2,1)}, u32[]{:S(2)}) copy-start(bf16[1,1024,2048]{2,1,0:T(8,128)(2,1)} %param.8) | copy-start | bytes 12582916
  578.8 18.5 %copy-start.2 = (f32[2048,256]{1,0:T(8,128)S(1)}, f32[2048,256]{1,0:T(8,128)}, u32[]{:S(2)}) copy-start(f32[2048,256]{1,0:T(8,128)} %all-gather.5.cloned.1.call-done) | copy-start | bytes 6291460
Sparse Core Ops, SparseCore 0:
  19.6 55.2 all-reduce.5
  79.1 54.8 all-reduce.7
  218.3 34.7 reduce-scatter.2
  254.6 28.5 all-gather.2
  305.0 53.0 all-reduce.9
  362.3 54.8 all-reduce.11
  501.4 34.7 reduce-scatter.4
  537.7 28.4 all-gather.4
where the time goes:
time: 626 us; the launch traced here: 621 us
  waiting for transfers between devices  288 us (46%)
  other arithmetic  114 us (18%)
  matrix products  109 us (17%)
  blocking collectives  78.7 us (13%)
  between operations  17.3 us (3%)
  local copies, waits for them, and re-layouts  11.9 us (2%)
    psum x2, waiting for transfers between devices, on_device(): gram_full = lax.psum(gram_part, 'row')  109 us
    psum x2, waiting for transfers between devices, on_device(): left = lax.psum(left_part, ('col', 'rep'))  109 us
    psum x2, blocking collectives, on_device(): lax.psum(jnp.sum(wide_piece * wide_piece, axis=0), ('row', 'col', 'rep'))  78.7 us
    reduce_scatter x2, waiting for transfers between devices, on_device(): lax.psum_scatter(factor_part, ('row', 'rep'), scatter_dimension=0, tiled=...  69.7 us
    another operation x13, other arithmetic, on_device(): low_factor = jnp.linalg.cholesky(gram_full)  68.6 us
    another operation x5, other arithmetic, on_device(): ortho = jax.scipy.linalg.solve_triangular(low_factor, left.T, lower=True).T  39.4 us
    dot_general x2, matrix products, on_device(): jnp.dot(buffer.T, ortho, precision=highest, preferred_element_type=jnp.fl...  34.4 us
    dot_general x2, matrix products, on_device(): jnp.dot(buffer, basis_now, precision=highest, preferred_element_type=jnp....  22.3 us
  transfers between devices with their start and end apart: 8, of which 6 were waited for; matrix products, arithmetic and copies ran while one was open for 0% of the time, Pallas kernels for 0%

commit v1 on v0

v1 whole, which is shorter than its diff:
```python
import jax
import jax.numpy as jnp
from jax import lax
from jax.experimental import pallas as pl
from jax.experimental.pallas import tpu as pltpu
from jax.sharding import PartitionSpec as P

D = 8192
RANK = 256
ITERS = 2
HALF = RANK // 2
SUB = 8

beta_mom = 0.95
learn_rate = 0.05

HIGHEST = lax.Precision.HIGHEST
HIGH = lax.Precision.HIGH


def dot(a, b, dims=((1,), (0,)), precision=HIGH):
    return lax.dot_general(a, b, (dims, ((), ())), precision=precision, preferred_element_type=jnp.float32)


def inverse_factor(block):
    lanes = lax.broadcasted_iota(jnp.int32, (SUB, HALF), 1)
    subs = lax.broadcasted_iota(jnp.int32, (SUB, HALF), 0)
    tiles = [block[SUB * i:SUB * (i + 1), :] for i in range(HALF // SUB)]
    for k in range(HALF):
        t, s = divmod(k, SUB)
        row = jnp.broadcast_to(tiles[t][s:s + 1, :], (SUB, HALF))
        r = lax.rsqrt(jnp.broadcast_to(row[:, k:k + 1], (SUB, HALF)))
        here = lanes == k
        scaled = jnp.where(here, r, row * r)
        for i in range(t, HALF // SUB):
            mult = jnp.broadcast_to(tiles[i][:, k:k + 1], (SUB, HALF)) * r
            base = jnp.where(here, 0.0, tiles[i])
            new = base - mult * scaled
            if i == t:
                new = jnp.where(subs > s, new, jnp.where(subs == s, scaled, tiles[i]))
            tiles[i] = new
    full = jnp.concatenate(tiles, axis=0)
    rows = lax.broadcasted_iota(jnp.int32, (HALF, HALF), 0)
    cols = lax.broadcasted_iota(jnp.int32, (HALF, HALF), 1)
    return jnp.where(cols <= rows, full, 0.0)


def inverse_kernel(gram_ref, out_ref):
    first = inverse_factor(gram_ref[:HALF, :HALF])
    side = dot(gram_ref[HALF:, :HALF], first, ((1,), (1,)), HIGHEST)
    rest = gram_ref[HALF:, HALF:] - dot(side, side, ((1,), (1,)), HIGHEST)
    second = inverse_factor(rest)
    out_ref[:HALF, :HALF] = first
    out_ref[:HALF, HALF:] = jnp.zeros((HALF, HALF), jnp.float32)
    out_ref[HALF:, :HALF] = -dot(second, dot(side, first, precision=HIGHEST), precision=HIGHEST)
    out_ref[HALF:, HALF:] = second


def inverse_cholesky(gram):
    return pl.pallas_call(
        inverse_kernel,
        out_shape=jax.ShapeDtypeStruct((RANK, RANK), jnp.float32),
        in_specs=[pl.BlockSpec(memory_space=pltpu.VMEM)],
        out_specs=pl.BlockSpec(memory_space=pltpu.VMEM),
        cost_estimate=pl.CostEstimate(flops=20_000_000_000, bytes_accessed=2 * 4 * RANK * RANK, transcendentals=RANK),
        name="inverse_cholesky",
    )(gram)


def swap(x, axis, bit):
    size = lax.axis_size(axis)
    return lax.ppermute(x, axis, [(i, i ^ bit) for i in range(size)])


def four_sum(x, axis, bits):
    one, two = bits
    return (x + swap(x, axis, one)) + (swap(x, axis, two) + swap(x, axis, one ^ two))


def left_sum(x):
    if lax.axis_size("col") != 4 or lax.axis_size("rep") != 1:
        return lax.psum(x, ("col", "rep"))
    half = x.shape[0] // 2
    up, low = x[:half], x[half:]
    up = up + swap(up, "col", 1)
    low = low + swap(low, "col", 2)
    up = up + swap(up, "col", 2)
    low = low + swap(low, "col", 1)
    return jnp.concatenate([up, low], axis=0)


def gram_sum(left):
    if lax.axis_size("col") != 4 or lax.axis_size("row") != 8:
        return lax.psum(dot(left, left, ((0,), (0,)), HIGHEST), "row")
    quarter = RANK // 4
    me = lax.axis_index("col")
    mine = lax.dynamic_slice_in_dim(left, me * quarter, quarter, axis=1)
    part = dot(mine, left, ((0,), (0,)), HIGHEST)
    part = part + swap(part, "row", 1)
    part = four_sum(part, "row", (2, 4))
    whole = jnp.zeros((4, quarter, RANK), jnp.float32)
    for bit in range(4):
        piece = part if bit == 0 else swap(part, "col", bit)
        whole = lax.dynamic_update_slice(whole, piece[None], (me ^ bit, 0, 0))
    return whole.reshape(RANK, RANK)


CHUNKS = 4


def factor_sum(x):
    if lax.axis_size("row") != 8 or lax.axis_size("rep") != 1:
        return lax.psum(x, ("row", "rep"))
    n = x.shape[1]
    me = lax.axis_index("row")
    core = me % 2
    rows = HALF // CHUNKS
    middle = jnp.logical_or(me // 2 == 1, me // 2 == 2)
    halves = x.reshape(2, CHUNKS, rows, n)
    kept = lax.dynamic_index_in_dim(halves, core, 0, keepdims=False)
    given = lax.dynamic_index_in_dim(halves, 1 - core, 0, keepdims=False)
    inward = [(0, 2), (1, 3), (6, 4), (7, 5)]
    across = [(2, 4), (3, 5), (4, 2), (5, 3)]
    outward = [(2, 0), (3, 1), (4, 6), (5, 7)]
    done = []
    for c in range(CHUNKS):
        part = kept[c] + swap(given[c], "row", 1)
        side = part + lax.ppermute(part, "row", inward)
        total = side + lax.ppermute(side, "row", across)
        done.append(jnp.where(middle, total, lax.ppermute(total, "row", outward)))
    mine = jnp.concatenate(done, axis=0)
    other = swap(mine, "row", 1)
    low = jnp.where(core == 0, mine, other)
    high = jnp.where(core == 0, other, mine)
    return jnp.concatenate([low, high], axis=0)


def column_sum(x):
    if lax.axis_size("col") != 4:
        return lax.psum(x, "col")
    return four_sum(x, "col", (1, 2))


def on_device(momentum, gradient, weight, right_basis):
    replicas = lax.axis_size("rep")
    buffer = momentum[0] + gradient[0].astype(jnp.float32)
    left_part = dot(buffer, right_basis) / replicas
    rms = None
    for sweep in range(ITERS):
        left = left_sum(left_part)
        if sweep:
            left = left / rms
        gram = gram_sum(left)
        wide = factor_sum(dot(left, buffer, ((0,), (0,))) / replicas)
        inverse = inverse_cholesky(gram)
        factor_t = dot(inverse, wide, precision=HIGHEST)
        square_sum = column_sum(jnp.sum(factor_t * factor_t, axis=1)[None, :])
        rms = jnp.sqrt(square_sum / jnp.float32(D) + 1e-06)
        if sweep < ITERS - 1:
            left_part = dot(buffer, factor_t, ((1,), (1,))) / replicas
    ortho = dot(left, inverse, ((1,), (1,)), HIGHEST)
    feedback = dot(ortho, factor_t)
    new_momentum = (buffer - (1.0 - beta_mom) * feedback)[None]
    basis_t = factor_t / rms.T
    update = dot(ortho, basis_t)
    new_weight = weight - learn_rate * jnp.sqrt(jnp.float32(D) / jnp.float32(RANK)) * update
    return (new_momentum, new_weight, basis_t.T)


def solution(mesh):
    return jax.shard_map(
        on_device,
        mesh=mesh,
        in_specs=(P("rep", "row", "col"), P("rep", "row", "col"), P("row", "col"), P("col", None)),
        out_specs=(P("rep", "row", "col"), P("row", "col"), P("col", None)),
        check_vma=False,
    )
```

time: 626 us -> 338 us (0.54)
  waiting for transfers between devices: 288 us -> 115 us
  other arithmetic: 114 us -> 7.92 us
  blocking collectives: 78.7 us -> 0 us
  Pallas kernels: 0 us -> 73.3 us
  starting transfers between devices: 0.83 us -> 72.6 us
  matrix products: 109 us -> 52.6 us
  between operations: 17.3 us -> 2.01 us
    psum x4 -> x0, waiting for transfers between devices: 218 us -> none  [the longest x2 109 us: on_device(): gram_full = lax.psum(gram_part, 'row')]
    ppermute x0 -> x62, waiting for transfers between devices: none -> 115 us  [the longest x38 48.7 us: swap(): return lax.ppermute(x, axis, [(i, i ^ bit) for i in range(size)])]
    another operation x18 -> x0, other arithmetic: 108 us -> none  [the longest x13 68.6 us: on_device(): low_factor = jnp.linalg.cholesky(gram_full)]
    psum x2 -> x0, blocking collectives: 78.7 us -> none  [on_device(): lax.psum(jnp.sum(wide_piece * wide_piece, axis=0), ('row', 'col', 'rep'))]
    pallas_call x0 -> x2, Pallas kernels: none -> 73.3 us  [inverse_cholesky(): pl.pallas_call(inverse_kernel, out_shape=jax.ShapeDtypeStruct((RANK, RANK...]
    ppermute x0 -> x62, starting transfers between devices: none -> 72.6 us  [the longest x38 39.3 us: swap(): return lax.ppermute(x, axis, [(i, i ^ bit) for i in range(size)])]
    reduce_scatter x2 -> x0, waiting for transfers between devices: 69.7 us -> none  [on_device(): lax.psum_scatter(factor_part, ('row', 'rep'), scatter_dimension=0, tiled=...]
    dot_general x8 -> x11, matrix products: 99.7 us -> 52.6 us  [dot(): lax.dot_general(a, b, (dims, ((), ())), precision=precision, preferred_el...]
  transfers between devices with their start and end apart: 8 -> 62, of which waited for: 6 -> 27; matrix products, arithmetic and copies ran while one was open for 0% -> 5% of each run, Pallas kernels for 0% -> 22%
where the time goes in v1:
time: 338 us; the launch traced here: 331 us
  waiting for transfers between devices  115 us (34%)
  Pallas kernels  73.3 us (22%)
  starting transfers between devices  72.6 us (21%)
  matrix products  52.6 us (16%)
  other arithmetic  7.92 us (2%)
  local copies, waits for them, and re-layouts  7.39 us (2%)
    pallas_call x2, Pallas kernels, inverse_cholesky(): pl.pallas_call(inverse_kernel, out_shape=jax.ShapeDtypeStruct((RANK, RANK...  73.3 us
    dot_general x11, matrix products, dot(): lax.dot_general(a, b, (dims, ((), ())), precision=precision, preferred_el...  52.6 us
    ppermute x38, waiting for transfers between devices, swap(): return lax.ppermute(x, axis, [(i, i ^ bit) for i in range(size)])  48.7 us
    ppermute x8, waiting for transfers between devices, factor_sum(): done.append(jnp.where(middle, total, lax.ppermute(total, 'row', outward)))  48.6 us
    ppermute x38, starting transfers between devices, swap(): return lax.ppermute(x, axis, [(i, i ^ bit) for i in range(size)])  39.3 us
    ppermute x8, waiting for transfers between devices, factor_sum(): side = part + lax.ppermute(part, 'row', inward)  18.2 us
    ppermute x8, starting transfers between devices, factor_sum(): side = part + lax.ppermute(part, 'row', inward)  17.1 us
    ppermute x8, starting transfers between devices, factor_sum(): done.append(jnp.where(middle, total, lax.ppermute(total, 'row', outward)))  10.8 us
  transfers between devices with their start and end apart: 62, of which 27 were waited for; matrix products, arithmetic and copies ran while one was open for 5% of the time, Pallas kernels for 22%

profile of v1, /device:TPU:0, one launch (start us, length us, event | category | flops | bytes accessed | tf_op | source)
XLA Modules:
  0.0 331.2 jit_solution(5949114436385945275)
XLA Ops:
  2.2 6.7 %fusion.6 = f32[1024,256]{1,0:T(8,128)S(1)} fusion(f32[2048,256]{1,0:T(8,128)S(1)} %copy-done, f32[1,1024,2048]{2,1,0:T(8,128)} %param.4, bf16[1,1024,2048]{2,1,0:T(8,128)(2,1)} %param.5), kind=kOutput, calls=%fused_computation.7 | convolution fusion | flops 3225419776 | bytes 15728640 | tf_op jit(solution)/shard_map/dot_general | solution.py:22
  13.6 10.4 %collective-permute-done = f32[512,256]{1,0:T(8,128)S(1)} collective-permute-done((f32[512,256]{1,0:T(8,128)S(1)}, f32[512,256]{1,0:T(8,128)S(1)}, u32[]{:S(2)}, u32[]{:S(2)}) %collective-permute-start) | collective-permute-done | bytes 524320 | tf_op jit(solution)/shard_map/ppermute | solution.py:72
  27.7 10.4 %collective-permute-done.3 = f32[512,256]{1,0:T(8,128)S(1)} collective-permute-done((f32[512,256]{1,0:T(8,128)S(1)}, f32[512,256]{1,0:T(8,128)S(1)}, u32[]{:S(2)}, u32[]{:S(2)}) %collective-permute-start.3) | collective-permute-done | bytes 524320 | tf_op jit(solution)/shard_map/ppermute | solution.py:72
  40.0 7.1 %fusion.2 = f32[2,4,32,2048]{3,2,1,0:T(8,128)S(1)} fusion(f32[2,4,32,1024]{3,2,1,0:T(8,128)} %bitcast.110, f32[1,1024,2048]{2,1,0:T(8,128)} %param.4, bf16[1,1024,2048]{2,1,0:T(8,128)(2,1)} %param.5), kind=kOutput, calls=%fused_computation.2 | convolution fusion | flops 3225419776 | bytes 15728640 | tf_op jit(solution)/shard_map/dot_general | solution.py:22
  57.0 3.6 %collective-permute-start.24 = (f32[32,2048]{1,0:T(8,128)S(1)}, f32[32,2048]{1,0:T(8,128)S(1)}, u32[]{:S(2)}, u32[]{:S(2)}) collective-permute-start(f32[32,2048]{1,0:T(8,128)S(1)} %get-tuple-element.28), channel_id=1, source_target_pairs={{0,8},{4,12},{24,16},{28,20},{1,9},{5,13},{25,17},{29,21},{2,10},{... | collective-permute-start | bytes 786440 | tf_op jit(solution)/shard_map/ppermute | solution.py:128
  78.6 4.0 %collective-permute-done.12 = f32[32,2048]{1,0:T(8,128)S(1)} collective-permute-done((f32[32,2048]{1,0:T(8,128)S(1)}, f32[32,2048]{1,0:T(8,128)S(1)}, u32[]{:S(2)}, u32[]{:S(2)}) %collective-permute-start.12) | collective-permute-done | bytes 262176 | tf_op jit(solution)/shard_map/ppermute | solution.py:128
  89.6 9.9 %collective-permute-done.26 = f32[32,2048]{1,0:T(8,128)S(1)} collective-permute-done((f32[32,2048]{1,0:T(8,128)S(1)}, f32[32,2048]{1,0:T(8,128)S(1)}, u32[]{:S(2)}, u32[]{:S(2)}) %collective-permute-start.26) | collective-permute-done | bytes 262176 | tf_op jit(solution)/shard_map/ppermute | solution.py:130
  99.5 5.6 %collective-permute-done.22 = f32[32,2048]{1,0:T(8,128)S(1)} collective-permute-done((f32[32,2048]{1,0:T(8,128)S(1)}, f32[32,2048]{1,0:T(8,128)S(1)}, u32[]{:S(2)}, u32[]{:S(2)}) %collective-permute-start.22) | collective-permute-done | bytes 262176 | tf_op jit(solution)/shard_map/ppermute | solution.py:130
  105.1 5.6 %collective-permute-done.18 = f32[32,2048]{1,0:T(8,128)S(1)} collective-permute-done((f32[32,2048]{1,0:T(8,128)S(1)}, f32[32,2048]{1,0:T(8,128)S(1)}, u32[]{:S(2)}, u32[]{:S(2)}) %collective-permute-start.18) | collective-permute-done | bytes 262176 | tf_op jit(solution)/shard_map/ppermute | solution.py:130
  110.8 3.4 %collective-permute-done.14 = f32[32,2048]{1,0:T(8,128)S(1)} collective-permute-done((f32[32,2048]{1,0:T(8,128)S(1)}, f32[32,2048]{1,0:T(8,128)S(1)}, u32[]{:S(2)}, u32[]{:S(2)}) %collective-permute-start.14) | collective-permute-done | bytes 262176 | tf_op jit(solution)/shard_map/ppermute | solution.py:130
  114.4 36.7 %inverse_cholesky.2 = f32[256,256]{1,0:T(8,128)} custom-call(f32[256,256]{1,0:T(8,128)} %bitcast.113), custom_call_target="tpu_custom_call" | custom-call | flops 20000000000 | bytes 524288 | tf_op jit(solution)/shard_map/inverse_cholesky/pallas_call | solution.py:60
  155.7 6.6 %fusion.4 = f32[1024,256]{1,0:T(8,128)S(1)} fusion(f32[256,2048]{1,0:T(8,128)S(1)} %get-tuple-element.42, f32[1,1024,2048]{2,1,0:T(8,128)} %param.4, bf16[1,1024,2048]{2,1,0:T(8,128)(2,1)S(1)} %copy-done.2), kind=kOutput, calls=%fused_computation.4 | convolution fusion | flops 3225419776 | bytes 15728640 | tf_op jit(solution)/shard_map/dot_general | solution.py:22
  165.3 11.4 %collective-permute-done.28 = f32[512,256]{1,0:T(8,128)S(1)} collective-permute-done((f32[512,256]{1,0:T(8,128)S(1)}, f32[512,256]{1,0:T(8,128)S(1)}, u32[]{:S(2)}, u32[]{:S(2)}) %collective-permute-start.28) | collective-permute-done | bytes 524320 | tf_op jit(solution)/shard_map/ppermute | solution.py:72
  183.7 8.0 %collective-permute-done.33 = f32[1,256]{1,0:T(1,128)S(1)} collective-permute-done((f32[1,256]{1,0:T(1,128)S(1)}, f32[1,256]{1,0:T(1,128)S(1)}, u32[]{:S(2)}, u32[]{:S(2)}) %collective-permute-start.33) | collective-permute-done | bytes 1056 | tf_op jit(solution)/shard_map/ppermute | solution.py:72
  192.8 6.9 %fusion = f32[2,4,32,2048]{3,2,1,0:T(8,128)S(1)} fusion(f32[2,4,32,1024]{3,2,1,0:T(8,128)S(1)} %bitcast.111, f32[1,1024,2048]{2,1,0:T(8,128)} %param.4, bf16[1,1024,2048]{2,1,0:T(8,128)(2,1)} %param.5), kind=kOutput, calls=%fused_computation | convolution fusion | flops 3225419776 | bytes 15728640 | tf_op jit(solution)/shard_map/dot_general | solution.py:22
  207.1 3.2 collective-permute-start.55
  224.5 4.0 %collective-permute-done.47 = f32[32,2048]{1,0:T(8,128)S(1)} collective-permute-done((f32[32,2048]{1,0:T(8,128)S(1)}, f32[32,2048]{1,0:T(8,128)S(1)}, u32[]{:S(2)}, u32[]{:S(2)}) %collective-permute-start.47) | collective-permute-done | bytes 262176 | tf_op jit(solution)/shard_map/ppermute | solution.py:128
  229.3 3.7 %collective-permute-done.43 = f32[32,2048]{1,0:T(8,128)S(1)} collective-permute-done((f32[32,2048]{1,0:T(8,128)S(1)}, f32[32,2048]{1,0:T(8,128)S(1)}, u32[]{:S(2)}, u32[]{:S(2)}) %collective-permute-start.43) | collective-permute-done | bytes 262176 | tf_op jit(solution)/shard_map/ppermute | solution.py:128
  240.1 9.8 %collective-permute-done.57 = f32[32,2048]{1,0:T(8,128)S(1)} collective-permute-done((f32[32,2048]{1,0:T(8,128)S(1)}, f32[32,2048]{1,0:T(8,128)S(1)}, u32[]{:S(2)}, u32[]{:S(2)}) %collective-permute-start.57) | collective-permute-done | bytes 262176 | tf_op jit(solution)/shard_map/ppermute | solution.py:130
  249.9 5.6 %collective-permute-done.53 = f32[32,2048]{1,0:T(8,128)S(1)} collective-permute-done((f32[32,2048]{1,0:T(8,128)S(1)}, f32[32,2048]{1,0:T(8,128)S(1)}, u32[]{:S(2)}, u32[]{:S(2)}) %collective-permute-start.53) | collective-permute-done | bytes 262176 | tf_op jit(solution)/shard_map/ppermute | solution.py:130
  255.5 5.6 %collective-permute-done.49 = f32[32,2048]{1,0:T(8,128)S(1)} collective-permute-done((f32[32,2048]{1,0:T(8,128)S(1)}, f32[32,2048]{1,0:T(8,128)S(1)}, u32[]{:S(2)}, u32[]{:S(2)}) %collective-permute-start.49) | collective-permute-done | bytes 262176 | tf_op jit(solution)/shard_map/ppermute | solution.py:130
  264.5 36.7 %inverse_cholesky.3 = f32[256,256]{1,0:T(8,128)} custom-call(f32[256,256]{1,0:T(8,128)} %bitcast.112), custom_call_target="tpu_custom_call" | custom-call | flops 20000000000 | bytes 524288 | tf_op jit(solution)/shard_map/inverse_cholesky/pallas_call | solution.py:60
  310.4 9.2 %fusion.8 = f32[1,1024,2048]{2,1,0:T(8,128)} fusion(f32[1024,256]{1,0:T(8,128)S(1)} %fusion.39, f32[256,2048]{1,0:T(8,128)S(1)} %get-tuple-element.44, f32[1,1024,2048]{2,1,0:T(8,128)} %param.4, bf16[1,1024,2048]{2,1,0:T(8,128)(2,1)S(1)} %copy-done.3), kind=kOutput, calls=%fused_computation.9 | convolution fusion | flops 3229614080 | bytes 24117248 | tf_op jit(solution)/shard_map/dot_general | solution.py:22
  321.3 6.6 %multiply_subtract_fusion = f32[1024,2048]{1,0:T(8,128)} fusion(f32[1024,2048]{1,0:T(8,128)S(1)} %bitcast.109, f32[1024,256]{1,0:T(8,128)S(1)} %fusion.39, f32[256,2048]{1,0:T(8,128)S(1)} %get-tuple-element.44, f32[256]{0:T(256)S(1)} %bitcast.115), kind=kOutput, calls=%fused_computation.10 | convolution fusion | flops 3225944064 | bytes 19923968 | tf_op jit(solution)/shard_map/dot_general | solution.py:22
  (192 shorter events, 108.7 us)
Async XLA Ops:
  9.0 14.9 %collective-permute-start = (f32[512,256]{1,0:T(8,128)S(1)}, f32[512,256]{1,0:T(8,128)S(1)}, u32[]{:S(2)}, u32[]{:S(2)}) collective-permute-start(f32[512,256]{1,0:T(8,128)S(1)} %get-tuple-element.39), channel_id=1, source_target_pairs={{0,1},{1,0},{2,3},{3,2},{4,5},{5,4},{6,7},{7,6},{8,9},{9,8},{10,11... | collective-permute-start | bytes 1572872 | tf_op jit(solution)/shard_map/ppermute | solution.py:72
  12.1 13.4 %collective-permute-start.2 = (f32[512,256]{1,0:T(8,128)S(1)}, f32[512,256]{1,0:T(8,128)S(1)}, u32[]{:S(2)}, u32[]{:S(2)}) collective-permute-start(f32[512,256]{1,0:T(8,128)S(1)} %get-tuple-element.40), channel_id=1, source_target_pairs={{0,2},{1,3},{2,0},{3,1},{4,6},{5,7},{6,4},{7,5},{8,10},{9,11},{10,... | collective-permute-start | bytes 1572872 | tf_op jit(solution)/shard_map/ppermute | solution.py:72
  64.9 13.0 %collective-permute-start.16 = (f32[32,2048]{1,0:T(8,128)S(1)}, f32[32,2048]{1,0:T(8,128)S(1)}, u32[]{:S(2)}, u32[]{:S(2)}) collective-permute-start(f32[32,2048]{1,0:T(8,128)S(1)} %get-tuple-element.27), channel_id=1, source_target_pairs={{0,8},{4,12},{24,16},{28,20},{1,9},{5,13},{25,17},{29,21},{2,10},{... | collective-permute-start | bytes 786440 | tf_op jit(solution)/shard_map/ppermute | solution.py:128
  66.2 16.4 %collective-permute-start.12 = (f32[32,2048]{1,0:T(8,128)S(1)}, f32[32,2048]{1,0:T(8,128)S(1)}, u32[]{:S(2)}, u32[]{:S(2)}) collective-permute-start(f32[32,2048]{1,0:T(8,128)S(1)} %get-tuple-element.25), channel_id=1, source_target_pairs={{0,8},{4,12},{24,16},{28,20},{1,9},{5,13},{25,17},{29,21},{2,10},{... | collective-permute-start | bytes 786440 | tf_op jit(solution)/shard_map/ppermute | solution.py:128
  67.6 15.7 %collective-permute-start.25 = (f32[32,2048]{1,0:T(8,128)S(1)}, f32[32,2048]{1,0:T(8,128)S(1)}, u32[]{:S(2)}, u32[]{:S(2)}) collective-permute-start(f32[32,2048]{1,0:T(8,128)S(1)} %add.216), channel_id=1, source_target_pairs={{8,16},{12,20},{16,8},{20,12},{9,17},{13,21},{17,9},{21,13},{10,18... | collective-permute-start | bytes 786440 | tf_op jit(solution)/shard_map/ppermute | solution.py:129
  68.3 15.7 %collective-permute-start.9 = (f32[64,256]{1,0:T(8,128)S(1)}, f32[64,256]{1,0:T(8,128)S(1)}, u32[]{:S(2)}, u32[]{:S(2)}) collective-permute-start(f32[64,256]{1,0:T(8,128)S(1)} %get-tuple-element.12), channel_id=1, source_target_pairs={{0,2},{1,3},{2,0},{3,1},{4,6},{5,7},{6,4},{7,5},{8,10},{9,11},{10,... | collective-permute-start | bytes 196616 | tf_op jit(solution)/shard_map/ppermute | solution.py:72
  72.3 13.1 %collective-permute-start.10 = (f32[64,256]{1,0:T(8,128)S(1)}, f32[64,256]{1,0:T(8,128)S(1)}, u32[]{:S(2)}, u32[]{:S(2)}) collective-permute-start(f32[64,256]{1,0:T(8,128)S(1)} %get-tuple-element.12), channel_id=1, source_target_pairs={{0,3},{1,2},{2,1},{3,0},{4,7},{5,6},{6,5},{7,4},{8,11},{9,10},{10,... | collective-permute-start | bytes 196616 | tf_op jit(solution)/shard_map/ppermute | solution.py:72
  84.0 15.5 %collective-permute-start.26 = (f32[32,2048]{1,0:T(8,128)S(1)}, f32[32,2048]{1,0:T(8,128)S(1)}, u32[]{:S(2)}, u32[]{:S(2)}) collective-permute-start(f32[32,2048]{1,0:T(8,128)S(1)} %add.217), channel_id=1, source_target_pairs={{8,0},{12,4},{16,24},{20,28},{9,1},{13,5},{17,25},{21,29},{10,2},{... | collective-permute-start | bytes 786440 | tf_op jit(solution)/shard_map/ppermute | solution.py:130
  85.4 19.7 %collective-permute-start.22 = (f32[32,2048]{1,0:T(8,128)S(1)}, f32[32,2048]{1,0:T(8,128)S(1)}, u32[]{:S(2)}, u32[]{:S(2)}) collective-permute-start(f32[32,2048]{1,0:T(8,128)S(1)} %add.214), channel_id=1, source_target_pairs={{8,0},{12,4},{16,24},{20,28},{9,1},{13,5},{17,25},{21,29},{10,2},{... | collective-permute-start | bytes 786440 | tf_op jit(solution)/shard_map/ppermute | solution.py:130
  86.8 23.9 %collective-permute-start.18 = (f32[32,2048]{1,0:T(8,128)S(1)}, f32[32,2048]{1,0:T(8,128)S(1)}, u32[]{:S(2)}, u32[]{:S(2)}) collective-permute-start(f32[32,2048]{1,0:T(8,128)S(1)} %add.211), channel_id=1, source_target_pairs={{8,0},{12,4},{16,24},{20,28},{9,1},{13,5},{17,25},{21,29},{10,2},{... | collective-permute-start | bytes 786440 | tf_op jit(solution)/shard_map/ppermute | solution.py:130
  88.1 26.1 %collective-permute-start.14 = (f32[32,2048]{1,0:T(8,128)S(1)}, f32[32,2048]{1,0:T(8,128)S(1)}, u32[]{:S(2)}, u32[]{:S(2)}) collective-permute-start(f32[32,2048]{1,0:T(8,128)S(1)} %add.208), channel_id=1, source_target_pairs={{8,0},{12,4},{16,24},{20,28},{9,1},{13,5},{17,25},{21,29},{10,2},{... | collective-permute-start | bytes 786440 | tf_op jit(solution)/shard_map/ppermute | solution.py:130
  114.3 36.8 %collective-permute-start.27 = (f32[128,2048]{1,0:T(8,128)S(1)}, f32[128,2048]{1,0:T(8,128)}, u32[]{:S(2)}, u32[]{:S(2)}) collective-permute-start(f32[128,2048]{1,0:T(8,128)S(1)} %pad_maximum_fusion.1), channel_id=1, source_target_pairs={{0,4},{4,0},{8,12},{12,8},{16,20},{20,16},{24,28},{28,24},{1,5},{5... | collective-permute-start | bytes 3145736 | tf_op jit(solution)/shard_map/ppermute | solution.py:72
  162.4 14.4 %collective-permute-start.28 = (f32[512,256]{1,0:T(8,128)S(1)}, f32[512,256]{1,0:T(8,128)S(1)}, u32[]{:S(2)}, u32[]{:S(2)}) collective-permute-start(f32[512,256]{1,0:T(8,128)S(1)} %get-tuple-element.35), channel_id=1, source_target_pairs={{0,1},{1,0},{2,3},{3,2},{4,5},{5,4},{6,7},{7,6},{8,9},{9,8},{10,11... | collective-permute-start | bytes 1572872 | tf_op jit(solution)/shard_map/ppermute | solution.py:72
  163.8 14.0 %collective-permute-start.30 = (f32[512,256]{1,0:T(8,128)S(1)}, f32[512,256]{1,0:T(8,128)S(1)}, u32[]{:S(2)}, u32[]{:S(2)}) collective-permute-start(f32[512,256]{1,0:T(8,128)S(1)} %get-tuple-element.36), channel_id=1, source_target_pairs={{0,2},{1,3},{2,0},{3,1},{4,6},{5,7},{6,4},{7,5},{8,10},{9,11},{10,... | collective-permute-start | bytes 1572872 | tf_op jit(solution)/shard_map/ppermute | solution.py:72
  178.0 14.3 %collective-permute-start.31 = (f32[512,256]{1,0:T(8,128)S(1)}, f32[512,256]{1,0:T(8,128)S(1)}, u32[]{:S(2)}, u32[]{:S(2)}) collective-permute-start(f32[512,256]{1,0:T(8,128)S(1)} %get-tuple-element.34), channel_id=1, source_target_pairs={{0,1},{1,0},{2,3},{3,2},{4,5},{5,4},{6,7},{7,6},{8,9},{9,8},{10,11... | collective-permute-start | bytes 1572872 | tf_op jit(solution)/shard_map/ppermute | solution.py:72
  178.7 13.6 %collective-permute-start.29 = (f32[512,256]{1,0:T(8,128)S(1)}, f32[512,256]{1,0:T(8,128)S(1)}, u32[]{:S(2)}, u32[]{:S(2)}) collective-permute-start(f32[512,256]{1,0:T(8,128)S(1)} %get-tuple-element.33), channel_id=1, source_target_pairs={{0,2},{1,3},{2,0},{3,1},{4,6},{5,7},{6,4},{7,5},{8,10},{9,11},{10,... | collective-permute-start | bytes 1572872 | tf_op jit(solution)/shard_map/ppermute | solution.py:72
  217.5 15.4 %collective-permute-start.43 = (f32[32,2048]{1,0:T(8,128)S(1)}, f32[32,2048]{1,0:T(8,128)S(1)}, u32[]{:S(2)}, u32[]{:S(2)}) collective-permute-start(f32[32,2048]{1,0:T(8,128)S(1)} %get-tuple-element.15), channel_id=1, source_target_pairs={{0,8},{4,12},{24,16},{28,20},{1,9},{5,13},{25,17},{29,21},{2,10},{... | collective-permute-start | bytes 786440 | tf_op jit(solution)/shard_map/ppermute | solution.py:128
  218.9 14.7 %collective-permute-start.56 = (f32[32,2048]{1,0:T(8,128)S(1)}, f32[32,2048]{1,0:T(8,128)S(1)}, u32[]{:S(2)}, u32[]{:S(2)}) collective-permute-start(f32[32,2048]{1,0:T(8,128)S(1)} %add.240), channel_id=1, source_target_pairs={{8,16},{12,20},{16,8},{20,12},{9,17},{13,21},{17,9},{21,13},{10,18... | collective-permute-start | bytes 786440 | tf_op jit(solution)/shard_map/ppermute | solution.py:129
  219.6 14.8 %collective-permute-start.40 = (f32[64,256]{1,0:T(8,128)S(1)}, f32[64,256]{1,0:T(8,128)S(1)}, u32[]{:S(2)}, u32[]{:S(2)}) collective-permute-start(f32[64,256]{1,0:T(8,128)S(1)} %get-tuple-element.10), channel_id=1, source_target_pairs={{0,2},{1,3},{2,0},{3,1},{4,6},{5,7},{6,4},{7,5},{8,10},{9,11},{10,... | collective-permute-start | bytes 196616 | tf_op jit(solution)/shard_map/ppermute | solution.py:72
  234.4 15.5 %collective-permute-start.57 = (f32[32,2048]{1,0:T(8,128)S(1)}, f32[32,2048]{1,0:T(8,128)S(1)}, u32[]{:S(2)}, u32[]{:S(2)}) collective-permute-start(f32[32,2048]{1,0:T(8,128)S(1)} %add.241), channel_id=1, source_target_pairs={{8,0},{12,4},{16,24},{20,28},{9,1},{13,5},{17,25},{21,29},{10,2},{... | collective-permute-start | bytes 786440 | tf_op jit(solution)/shard_map/ppermute | solution.py:130
  235.8 19.7 %collective-permute-start.53 = (f32[32,2048]{1,0:T(8,128)S(1)}, f32[32,2048]{1,0:T(8,128)S(1)}, u32[]{:S(2)}, u32[]{:S(2)}) collective-permute-start(f32[32,2048]{1,0:T(8,128)S(1)} %add.238), channel_id=1, source_target_pairs={{8,0},{12,4},{16,24},{20,28},{9,1},{13,5},{17,25},{21,29},{10,2},{... | collective-permute-start | bytes 786440 | tf_op jit(solution)/shard_map/ppermute | solution.py:130
  237.2 23.9 %collective-permute-start.49 = (f32[32,2048]{1,0:T(8,128)S(1)}, f32[32,2048]{1,0:T(8,128)S(1)}, u32[]{:S(2)}, u32[]{:S(2)}) collective-permute-start(f32[32,2048]{1,0:T(8,128)S(1)} %add.235), channel_id=1, source_target_pairs={{8,0},{12,4},{16,24},{20,28},{9,1},{13,5},{17,25},{21,29},{10,2},{... | collective-permute-start | bytes 786440 | tf_op jit(solution)/shard_map/ppermute | solution.py:130
  238.5 25.8 %collective-permute-start.45 = (f32[32,2048]{1,0:T(8,128)S(1)}, f32[32,2048]{1,0:T(8,128)S(1)}, u32[]{:S(2)}, u32[]{:S(2)}) collective-permute-start(f32[32,2048]{1,0:T(8,128)S(1)} %add.232), channel_id=1, source_target_pairs={{8,0},{12,4},{16,24},{20,28},{9,1},{13,5},{17,25},{21,29},{10,2},{... | collective-permute-start | bytes 786440 | tf_op jit(solution)/shard_map/ppermute | solution.py:130
  264.4 38.8 %collective-permute-start.58 = (f32[128,2048]{1,0:T(8,128)S(1)}, f32[128,2048]{1,0:T(8,128)}, u32[]{:S(2)}, u32[]{:S(2)}) collective-permute-start(f32[128,2048]{1,0:T(8,128)S(1)} %pad_maximum_fusion.2), channel_id=1, source_target_pairs={{0,4},{4,0},{8,12},{12,8},{16,20},{20,16},{24,28},{28,24},{1,5},{5... | collective-permute-start | bytes 3145736 | tf_op jit(solution)/shard_map/ppermute | solution.py:72
  (47 other events, 408.4 us)
